TPU v7x, 32 devices: a whole 2x2x4 slice. The times are simulated.
32 devices in a mesh: cls: 4 (over z), vol: 8 (over y, x, core).
Axes of the slice: x: 2, y: 2, z: 4, core: 2. Of those that a mesh axis runs over, the one named last changes fastest.
Arguments:
- images: bfloat16 [256, 256, 2, 256], P(('cls', 'vol')), may hold values from -8 to 8
- projections: bfloat16 [4, 128, 256, 2, 256], P('cls', None, 'vol'), may hold values from -0.049718446 to 0.049718446
- assignment: int32 [256, 1], P(('cls', 'vol')), may hold values from 0 to 3; in each aligned block of 8 rows (0 to 7, 8 to 15, ...) at most 4 rows name the same one
- interp_cells: int32 [128, 4, 256], replicated, may hold values from 0 to 65535, as said below
- interp_weights: float32 [128, 4, 256], replicated, may hold values from 0 to 1, as said below
Outputs:
- class_volume: float32 [4, 256, 256, 256], P('cls', 'vol')
Inputs may be any that keep to these rules, and one draw needn't show every extreme that they name: `assignment`: among the 8 particles of one device (aligned blocks of 8 rows), at most 4 name the same class. `interp_cells`: for each direction and column u the four cells are (x, y), (x + 1, y), (x, y + 1), (x + 1, y + 1) modulo 256, in that order. `interp_weights`: for each direction and column u the four weights are nonnegative and sum to one.
All inputs are finite; a program needn't handle non-finite values.
Results may differ from a plain program's by a relative error of at most 0.0027.
Values may be sent and summed in bfloat16 or wider, within the bound.
No kernel may reach another device: no remote copies, remote signals or barrier semaphores. Data moves between devices by JAX's collectives and lax.ppermute only.
A program may use at most 256 MiB of HBM per device.

v0:
```python
import math

import jax
import jax.numpy as jnp
from jax import lax
from jax.sharding import PartitionSpec as P

PRECISE = lax.Precision.HIGHEST


def dft_tables(length):
    index = jnp.arange(length, dtype=jnp.int32)
    phase = index[:, None] * index[None, :] % length
    angle = phase.astype(jnp.float32) * (2.0 * math.pi / length)
    factor = 1.0 / math.sqrt(length)
    return (jnp.cos(angle) * factor, jnp.sin(angle) * factor)


def shards(images, projections, assignment, interp_cells, interp_weights):
    class_count = lax.axis_size("cls")
    slab_count = lax.axis_size("vol")
    local_count = images.shape[0]
    grid_side = images.shape[3]
    slab_rows = grid_side // slab_count
    row_width = slab_rows * 2 * grid_side
    capacity = 2 * local_count // class_count
    classes = assignment[:, 0]
    onehot = (classes[:, None] == jnp.arange(class_count, dtype=jnp.int32)[None, :]).astype(
        jnp.int32
    )
    before = jnp.cumsum(onehot, axis=0) - onehot
    slot_index = classes * capacity + jnp.sum(before * onehot, axis=1)
    slot_table = jnp.full((class_count * capacity,), local_count, jnp.int32)
    slot_table = (
        slot_table.at[slot_index]
        .set(jnp.arange(local_count, dtype=jnp.int32))
        .reshape(class_count, capacity)
    )
    blocks = images.reshape(local_count, slab_count, row_width)
    block_index = jnp.arange(slab_count, dtype=jnp.int32)
    outgoing = blocks.at[slot_table[:, None, :], block_index[None, :, None]].get(
        mode="fill", fill_value=0
    )
    arrived = lax.all_to_all(
        outgoing.reshape(class_count * slab_count, capacity, row_width),
        ("cls", "vol"),
        split_axis=0,
        concat_axis=0,
        tiled=True,
    )
    arrived = arrived.reshape(-1, row_width)
    references = projections.reshape(projections.shape[1], row_width)
    partial_value = jnp.einsum("sm,km->sk", arrived, references, preferred_element_type=jnp.float32)
    scores = lax.psum(partial_value, "vol")
    highest = jnp.max(scores, axis=1, keepdims=True)
    expo = jnp.exp(scores - highest)
    posterior = (expo / jnp.sum(expo, axis=1, keepdims=True)).astype(jnp.bfloat16)
    average = jnp.einsum("sk,sm->km", posterior, arrived, preferred_element_type=jnp.float32)
    spread = average.reshape(-1, slab_rows, 2, grid_side)
    contribution = (
        jnp.transpose(spread, (0, 3, 1, 2))[:, None, :, :, :] * interp_weights[:, :, :, None, None]
    )
    fourier_plane = jnp.zeros((grid_side * grid_side, slab_rows * 2), jnp.float32)
    fourier_plane = fourier_plane.at[interp_cells.reshape(-1)].add(
        contribution.reshape(-1, slab_rows * 2)
    )
    fourier_plane = jnp.transpose(
        fourier_plane.reshape(grid_side, grid_side, slab_rows, 2), (3, 2, 0, 1)
    )
    real_part = fourier_plane[0]
    imag_part = fourier_plane[1]
    cosine, sine_table = dft_tables(grid_side)
    real_next = jnp.einsum("zxy,yw->zxw", real_part, cosine, precision=PRECISE) - jnp.einsum(
        "zxy,yw->zxw", imag_part, sine_table, precision=PRECISE
    )
    imag_next = jnp.einsum("zxy,yw->zxw", real_part, sine_table, precision=PRECISE) + jnp.einsum(
        "zxy,yw->zxw", imag_part, cosine, precision=PRECISE
    )
    real_part = jnp.einsum("zxy,xw->zwy", real_next, cosine, precision=PRECISE) - jnp.einsum(
        "zxy,xw->zwy", imag_next, sine_table, precision=PRECISE
    )
    imag_part = jnp.einsum("zxy,xw->zwy", real_next, sine_table, precision=PRECISE) + jnp.einsum(
        "zxy,xw->zwy", imag_next, cosine, precision=PRECISE
    )
    real_piece = lax.all_to_all(real_part, "vol", split_axis=1, concat_axis=0, tiled=True)
    imag_piece = lax.all_to_all(imag_part, "vol", split_axis=1, concat_axis=0, tiled=True)
    volume = jnp.einsum("zxy,zw->xyw", real_piece, cosine, precision=PRECISE) - jnp.einsum(
        "zxy,zw->xyw", imag_piece, sine_table, precision=PRECISE
    )
    return volume[None]


def solution(mesh):
    in_specs = (
        P(("cls", "vol"), None, None, None),
        P("cls", None, "vol", None, None),
        P(("cls", "vol"), None),
        P(),
        P(),
    )
    out_specs = P("cls", "vol", None, None)
    return jax.shard_map(shards, mesh=mesh, in_specs=in_specs, out_specs=out_specs, check_vma=False)
```

profile of v0, /device:TPU:0, one launch (start us, length us, event | category | flops | bytes accessed | tf_op | source)
XLA Modules:
  0.0 1396.9 jit_solution(16685003614493376216)
XLA Ops:
  6.5 0.7 fusion.67
  7.2 0.2 reduce_window_sum.11
  7.4 0.7 select_reduce_fusion
  8.1 0.7 fusion.68
  8.7 0.6 scatter_custom_fusion
  9.5 3.3 reshape.79
  12.8 15.1 %gather_fusion = bf16[128,16384]{1,0:T(8,128)(2,1)} fusion(bf16[8,8,16384]{2,1,0:T(8,128)(2,1)S(1)} %reshape.79, s32[128]{0:T(128)S(1)} %reshape.83), kind=kCustom, calls=%fused_computation | custom fusion | bytes 8389632 | tf_op jit(solution)/shard_map/gather | solution.py:41
  28.0 7.2 gather.6
  35.2 6.0 broadcast_select_fusion
  41.3 7.4 all-to-all-start
  48.8 0.6 reshape.78
  49.4 7.8 reshape.81
  57.2 85.4 %all-to-all-done = bf16[32,4,16384]{2,1,0:T(4,128)(2,1)} async-done(((bf16[32,4,16384]{2,1,0:T(4,128)(2,1)}), bf16[32,4,16384]{2,1,0:T(4,128)(2,1)}, u32[]{:S(2)}, u32[]{:S(2)}) %all-to-all-start) | async-done | bytes 4194336 | tf_op jit(solution)/shard_map/all_to_all | solution.py:44
  142.6 6.9 reshape.80
  149.5 5.3 fusion.121
  154.8 0.5 compare_select_fusion
  155.4 0.3 copy.108
  155.7 6.4 copy.78
  162.1 44.8 %all-reduce.2.cloned.1.call-done = f32[128,128]{1,0:T(8,128)} async-done(((f32[128,128]{1,0:T(8,128)}), f32[128,128]{1,0:T(8,128)}) %all-reduce.2.cloned.1.call-update) | async-done | bytes 65552 | tf_op jit(solution)/shard_map/psum | solution.py:54
  206.8 0.9 reduce_max.9
  207.8 1.0 fusion.60
  208.8 7.0 convolution_bitcast_fusion
  215.8 13.6 mul.146
  229.4 30.6 %mul.147 = f32[131072,64]{0,1:T(8,128)} reshape(f32[128,4,256,32,2]{2,1,0,4,3:T(4,128)} %mul.146) | data formatting | bytes 67108864 | tf_op jit(solution)/shard_map/mul | solution.py:61
  259.9 22.3 %broadcast_multiply_fusion = f32[131072,64]{0,1:T(8,128)} fusion(f32[131072,64]{0,1:T(8,128)} %mul.147, f32[131072]{0:T(1024)S(1)} %bitcast.96), kind=kLoop, calls=%fused_computation.4 | loop fusion | flops 8388608 | bytes 67633152 | tf_op jit(solution)/shard_map/mul | solution.py:61
  282.2 44.2 %copy.80 = f32[131072,64]{1,0:T(8,128)} copy(f32[131072,64]{0,1:T(8,128)} %broadcast_multiply_fusion) | data formatting | bytes 67108864 | tf_op jit(solution)/shard_map/mul | solution.py:61
  326.4 707.1 %scatter_custom_fusion.1 = f32[65536,64]{1,0:T(8,128)} fusion(s32[131072]{0:T(1024)S(1)} %bitcast.98, f32[131072,64]{1,0:T(8,128)} %copy.80, f32[]{:T(128)} %constant.19.clone.1), kind=kCustom, calls=%fused_computation.5 | custom fusion | flops 8388608 | bytes 16777728 | tf_op jit(solution)/shard_map/scatter-add | solution.py:64
  1033.6 24.5 %copy.81 = f32[65536,64]{0,1:T(8,128)} copy(f32[65536,64]{1,0:T(8,128)} %scatter_custom_fusion.1) | data formatting | bytes 33554432 | tf_op jit(solution)/shard_map/scatter-add | solution.py:64
  1058.0 10.9 copy.109
  1068.9 1.9 copy.117
  1070.9 7.9 fusion.8
  1078.7 8.4 fusion.6
  1087.1 10.8 fusion.9
  1097.9 11.2 fusion.7
  1109.1 11.5 fusion.12
  1120.6 14.9 %subtract_bitcast_fusion.1 = f32[32,256,256]{2,1,0:T(8,128)S(1)} fusion(f32[256,32,256]{2,0,1:T(8,128)} %fusion.12, f32[32,256,256]{2,1,0:T(8,128)} %fusion.7, f32[32,256,256]{2,1,0:T(8,128)} %fusion.9), kind=kOutput, calls=%fused_computation.15 | convolution fusion | flops 6447628288 | bytes 33554432 | tf_op jit(solution)/shard_map/zxy,xw->zwy/dot_general | solution.py:79
  1135.5 8.1 copy.85
  1143.6 5.4 all-to-all-start.1
  1148.9 13.4 fusion.10
  1162.3 15.1 %add_bitcast_fusion = f32[32,256,256]{2,1,0:T(8,128)} fusion(f32[256,32,256]{2,0,1:T(8,128)S(1)} %fusion.10, f32[32,256,256]{2,1,0:T(8,128)} %fusion.7, f32[32,256,256]{2,1,0:T(8,128)} %fusion.9), kind=kOutput, calls=%fused_computation.14 | convolution fusion | flops 6447628288 | bytes 33554432 | tf_op jit(solution)/shard_map/zxy,xw->zwy/dot_general | solution.py:82
  1177.4 11.4 copy.91
  1188.9 54.1 %all-to-all-done.1 = f32[32,256,256]{2,0,1:T(8,128)} async-done(((f32[32,256,256]{2,0,1:T(8,128)}), f32[32,256,256]{2,0,1:T(8,128)}, u32[]{:S(2)}, u32[]{:S(2)}) %all-to-all-start.1) | async-done | bytes 8388640 | tf_op jit(solution)/shard_map/all_to_all | solution.py:85
  1243.0 5.1 all-to-all-start.2
  1248.2 11.6 copy.87
  1259.8 82.3 %all-to-all-done.2 = f32[32,256,256]{2,0,1:T(8,128)} async-done(((f32[32,256,256]{2,0,1:T(8,128)}), f32[32,256,256]{2,0,1:T(8,128)}, u32[]{:S(2)}, u32[]{:S(2)}) %all-to-all-start.2) | async-done | bytes 8388640 | tf_op jit(solution)/shard_map/all_to_all | solution.py:86
  1342.1 8.3 copy.93
  1350.3 19.3 %fusion.2 = f32[32,256,256]{2,1,0:T(8,128)S(1)} fusion(f32[256,32,256]{2,1,0:T(8,128)S(1)} %bitcast.94), kind=kOutput, calls=%fused_computation.9 | convolution fusion | flops 6443433984 | bytes 16777216 | tf_op jit(solution)/shard_map/zxy,zw->xyw/dot_general | solution.py:87
  1369.7 20.2 %subtract_bitcast_fusion = f32[1,32,256,256]{3,2,1,0:T(8,128)} fusion(f32[32,256,256]{2,1,0:T(8,128)S(1)} %fusion.2, f32[256,32,256]{2,1,0:T(8,128)S(1)} %bitcast.93), kind=kOutput, calls=%fused_computation.13 | convolution fusion | flops 6445531136 | bytes 25165824 | tf_op jit(solution)/shard_map/zxy,zw->xyw/dot_general | solution.py:87
  (23 shorter events, 0.3 us)
Async XLA Ops:
  35.2 13.5 copy-start.2
  41.3 101.3 %all-to-all-start = ((bf16[32,4,16384]{2,1,0:T(4,128)(2,1)}), bf16[32,4,16384]{2,1,0:T(4,128)(2,1)}, u32[]{:S(2)}, u32[]{:S(2)}) async-start(bf16[32,4,16384]{2,1,0:T(4,128)(2,1)} %broadcast_select_fusion), calls=%async_computation | async-start | bytes 8388608 | tf_op jit(solution)/shard_map/all_to_all | solution.py:44
  48.7 158.1 %all-reduce.2.cloned.1.call-start = ((), (), s32[]{:S(2)}) async-start(), calls=%async_computation.3 | async-start | bytes 131072 | tf_op jit(solution)/shard_map/psum | solution.py:54
  57.2 98.2 %copy-start.3 = (f32[128,4,256]{2,1,0:T(4,128)S(1)}, f32[128,4,256]{2,1,0:T(4,128)}, u32[]{:S(2)}) copy-start(f32[128,4,256]{2,1,0:T(4,128)} %param.9) | copy-start | bytes 1572868
  1078.7 30.4 %copy-start = (f32[32,256,256]{2,1,0:T(8,128)}, f32[32,256,256]{2,1,0:T(8,128)S(1)}, u32[]{:S(2)}) copy-start(f32[32,256,256]{2,1,0:T(8,128)S(1)} %fusion.8) | copy-start | bytes 25165828
  1087.1 22.0 %copy-start.1 = (f32[32,256,256]{2,1,0:T(8,128)}, f32[32,256,256]{2,1,0:T(8,128)S(1)}, u32[]{:S(2)}) copy-start(f32[32,256,256]{2,1,0:T(8,128)S(1)} %fusion.6) | copy-start | bytes 25165828
  1143.6 99.4 %all-to-all-start.1 = ((f32[32,256,256]{2,0,1:T(8,128)}), f32[32,256,256]{2,0,1:T(8,128)}, u32[]{:S(2)}, u32[]{:S(2)}) async-start(f32[32,256,256]{2,0,1:T(8,128)} %copy.85), calls=%async_computation.1 | async-start | bytes 16777216 | tf_op jit(solution)/shard_map/all_to_all | solution.py:85
  1243.0 99.0 %all-to-all-start.2 = ((f32[32,256,256]{2,0,1:T(8,128)}), f32[32,256,256]{2,0,1:T(8,128)}, u32[]{:S(2)}, u32[]{:S(2)}) async-start(f32[32,256,256]{2,0,1:T(8,128)} %copy.91), calls=%async_computation.2 | async-start | bytes 16777216 | tf_op jit(solution)/shard_map/all_to_all | solution.py:86
  1342.1 27.6 %slice-start = ((s8[8388608]{0:T(1024)(128)(4,1)}), s8[4194304]{0:T(1024)(128)(4,1)S(1)}, s32[]{:S(2)}) async-start(s8[8388608]{0:T(1024)(128)(4,1)} %bitcast.91), calls=%async_computation.4 | async-start | bytes 8388608
  1350.3 19.4 %slice-start.1 = ((s8[8388608]{0:T(1024)(128)(4,1)}), s8[4194304]{0:T(1024)(128)(4,1)S(1)}, s32[]{:S(2)}) async-start(s8[8388608]{0:T(1024)(128)(4,1)} %bitcast.91), calls=%async_computation.5 | async-start | bytes 8388608
Sparse Core Ops, SparseCore 0:
  154.9 51.8 all-reduce.1
where the time goes:
time: 1420 us; the launch traced here: 1400 us
  other arithmetic  740 us (52%)
  waiting for transfers between devices  267 us (19%)
  local copies, waits for them, and re-layouts  213 us (15%)
  matrix products  145 us (10%)
  starting transfers between devices  18 us (1%)
    scatter-add x1, other arithmetic, shards(): fourier_plane.at[interp_cells.reshape(-1)]  707 us
    mul x3, local copies, waits for them, and re-layouts, shards(): jnp.transpose(spread, (0, 3, 1, 2))[:, None, :, :, :]  88.4 us
    all_to_all x1, waiting for transfers between devices, shards(): lax.all_to_all(outgoing.reshape(class_count * slab_count, capacity, row_w...  85.4 us
    all_to_all x1, waiting for transfers between devices, shards(): lax.all_to_all(imag_part, 'vol', split_axis=1, concat_axis=0, tiled=True)  82.3 us
    all_to_all x1, waiting for transfers between devices, shards(): lax.all_to_all(real_part, 'vol', split_axis=1, concat_axis=0, tiled=True)  54.1 us
    psum x1, waiting for transfers between devices, shards(): scores = lax.psum(partial_value, 'vol')  44.8 us
  transfers between devices with their start and end apart: 4, of which 4 were waited for; matrix products, arithmetic and copies ran while one was open for 5% of the time, Pallas kernels for 0%

commit v1 on v0

v1 whole, which is shorter than its diff:
```python
import functools
import math

import jax
import jax.numpy as jnp
import numpy as np
from jax import lax
from jax.experimental import pallas as pl
from jax.experimental.pallas import tpu as pltpu
from jax.sharding import PartitionSpec as P

F32 = jnp.float32
BF16 = jnp.bfloat16
LANES = 128
HALF = 64
CHUNK = 128
VMEM = pltpu.VMEM


def split_table(table):
    high = table.astype(jnp.bfloat16)
    low = (table - high.astype(np.float64)).astype(jnp.bfloat16)
    return high, low


def tables(grid, slabs):
    half = grid // 2
    scale = 1.0 / math.sqrt(grid)
    index = np.arange(grid)
    angle = 2.0 * np.pi / grid
    phase = (index[:, None] * np.arange(half)[None, :]) % grid
    cosine = np.cos(phase * angle)
    sine = np.sin(phase * angle)
    sine[:, 0] = np.cos(((index * half) % grid) * angle)
    table_y = np.concatenate([cosine, sine], axis=1) * scale
    rows = half + 8
    phase = (np.arange(rows)[:, None] * index[None, :]) % grid
    live = (np.arange(rows) <= half)[:, None]
    table_x = np.concatenate([np.cos(phase * angle) * live, np.sin(phase * angle) * live], axis=0) * scale
    phase = (index[:, None] * index[None, :]) % grid
    table_z = np.stack([np.cos(phase * angle), -np.sin(phase * angle)], axis=1).reshape(2 * grid, grid) * scale
    order = np.concatenate([np.arange(half), [half], np.arange(grid - 1, half, -1)])
    restore = (order[None, :] == index[:, None]).astype(jnp.bfloat16)
    return split_table(table_y), split_table(table_x), split_table(table_z), restore


def dot(a, b):
    return jnp.dot(a, b, preferred_element_type=F32)


def dot_t(a, b):
    return lax.dot_general(a, b, (((1,), (1,)), ((), ())), preferred_element_type=F32)


def two_terms(value):
    high = value.astype(BF16)
    low = (value - high.astype(F32)).astype(BF16)
    return high, low


def score_kernel(cap, dirs, images_ref, refs_ref, out_ref, sums):
    sources, groups, rows16, _ = images_ref.shape
    rows = sources * rows16
    steps = rows16 // cap
    sums[...] = jnp.zeros_like(sums)

    def step(g, carry):
        block = images_ref[:, pl.ds(g, 1), :, :].reshape(rows, LANES)
        sums[...] += dot_t(refs_ref[g], block)
        return carry

    lax.fori_loop(0, groups, step, 0)
    column = lax.broadcasted_iota(jnp.int32, (dirs, rows), 1)
    part = (column & (rows16 - 1)) // cap
    kept = jnp.zeros((dirs, rows), F32)
    for j in range(steps):
        kept = kept + jnp.where(part == j, sums[j * dirs : (j + 1) * dirs, :], 0.0)
    slots = sources * cap
    row_id = lax.broadcasted_iota(jnp.int32, (rows, slots), 0)
    slot_id = lax.broadcasted_iota(jnp.int32, (rows, slots), 1)
    gather = (row_id // rows16 * cap + row_id % cap) == slot_id
    out_ref[...] = jnp.dot(
        kept, gather.astype(F32), preferred_element_type=F32, precision=lax.Precision.HIGHEST
    )


def scores_call(images, refs, cap, dirs):
    sources, groups, rows16, _ = images.shape
    return pl.pallas_call(
        functools.partial(score_kernel, cap, dirs),
        out_shape=jax.ShapeDtypeStruct((dirs, sources * cap), F32),
        in_specs=[pl.BlockSpec(memory_space=VMEM)] * 2,
        out_specs=pl.BlockSpec(memory_space=VMEM),
        scratch_shapes=[VMEM((refs.shape[1], sources * rows16), F32)],
        compiler_params=pltpu.CompilerParams(vmem_limit_bytes=48 * 2**20),
        name="scores",
    )(images, refs)


def scatter_kernel(
    cap,
    width,
    grid,
    total_ref,
    chunk_row_ref,
    chunk_start_ref,
    point_ref,
    parts_ref,
    images_ref,
    weights_ref,
    keys_ref,
    out_ref,
    values,
    buffer_a,
    buffer_b,
    sums,
    spread,
):
    sources, groups, rows16, _ = images_ref.shape
    rows = sources * rows16
    steps = rows16 // cap
    dirs, slots = parts_ref.shape[1:]
    joined = steps * dirs
    halves = LANES // width

    total = parts_ref[0]
    for i in range(1, parts_ref.shape[0]):
        total = total + parts_ref[i]
    expo = jnp.exp(total - jnp.max(total, axis=0, keepdims=True))
    posterior = (expo / jnp.sum(expo, axis=0, keepdims=True)).astype(BF16)
    slot_id = lax.broadcasted_iota(jnp.int32, (slots, rows), 0)
    row_id = lax.broadcasted_iota(jnp.int32, (slots, rows), 1)
    repeat = ((row_id // rows16 * cap + row_id % cap) == slot_id).astype(F32).astype(BF16)
    wide = dot(posterior, repeat)
    part = (lax.broadcasted_iota(jnp.int32, (dirs, rows), 1) & (rows16 - 1)) // cap
    for j in range(steps):
        spread[j * dirs : (j + 1) * dirs, :] = jnp.where(part == j, wide, 0.0).astype(BF16)

    lane_j = lax.broadcasted_iota(jnp.int32, (joined, LANES), 1)

    def average(g, carry):
        block = images_ref[:, pl.ds(g, 1), :, :].reshape(rows, LANES)
        mean = dot(spread[...], block)
        weight = weights_ref[g]
        for h in range(halves):
            shifted = mean if h == 0 else pltpu.roll(mean, LANES - h * width, 1)
            behind = pltpu.roll(weight, HALF - 4 * h, 1)
            start = pl.multiple_of((h * groups + g) * joined, joined)
            values[pl.ds(start, joined), :] = jnp.where(lane_j < HALF, shifted, behind)
        return carry

    lax.fori_loop(0, groups, average, 0)

    buffer_a[...] = jnp.zeros_like(buffer_a)
    buffer_b[...] = jnp.zeros_like(buffer_b)
    sums[...] = jnp.zeros_like(sums)

    lane = lax.broadcasted_iota(jnp.int32, (CHUNK, LANES), 1)
    lane_y = lax.broadcasted_iota(jnp.int32, (grid, LANES), 1)
    cell_y = lax.broadcasted_iota(jnp.int32, (grid, CHUNK), 0)
    lane_8 = lax.broadcasted_iota(jnp.int32, (8, LANES), 1)
    pick_row = lax.broadcasted_iota(jnp.int32, (width, LANES), 0)
    pick_lane = lax.broadcasted_iota(jnp.int32, (width, LANES), 1)
    pick = ((pick_lane == pick_row) | (pick_lane == pick_row + HALF)).astype(F32).astype(BF16)

    def fetch(c, buffer):
        start = chunk_start_ref[c]
        for i in range(CHUNK):
            buffer[pl.ds(i, 1), :] = values[pl.ds(point_ref[start + i], 1), :]

    def transposed(plane):
        high = plane.astype(BF16).astype(F32)
        both = jnp.where(lane_y < HALF, high, pltpu.roll(plane - high, HALF, 1)).astype(BF16)
        return dot_t(pick, both)

    def put(x, flipped):
        for side in range(grid // LANES):
            out_ref[side, pl.ds(x, width, stride=grid), :] = flipped[:, side * LANES : (side + 1) * LANES]

    def work(c, buffer):
        row = chunk_row_ref[c]
        before = chunk_row_ref[jnp.maximum(c - 1, 0)]
        start = chunk_start_ref[c]
        base = start >> 7
        offset = start & (LANES - 1)
        turn = LANES - offset
        first = pltpu.roll(jnp.broadcast_to(keys_ref[pl.ds(base, 1), :], (8, LANES)), turn, 1)
        second = pltpu.roll(jnp.broadcast_to(keys_ref[pl.ds(base + 1, 1), :], (8, LANES)), turn, 1)
        key = jnp.where(lane_8 < turn, first, second)
        valid = (key >> 23) == row
        y = (key >> 15) & (grid - 1)
        low_y = jnp.where(valid, y, -1)[0:1, :]
        high_y = jnp.where(valid, (y + 1) & (grid - 1), -1)[0:1, :]
        hot = jnp.concatenate(
            [
                jnp.where(cell_y == low_y, 1.0, 0.0).astype(BF16),
                jnp.where(cell_y == high_y, 1.0, 0.0).astype(BF16),
            ],
            axis=1,
        )
        data = buffer[...]
        twice = jnp.where(lane < HALF, data, pltpu.roll(data, HALF, 1))
        weight = [jnp.broadcast_to(data[:, HALF + j : HALF + j + 1], (CHUNK, LANES)) for j in range(4)]
        low_h, low_l = two_terms(twice * jnp.where(lane < HALF, weight[0], weight[1]))
        high_h, high_l = two_terms(twice * jnp.where(lane < HALF, weight[2], weight[3]))
        operand = jnp.concatenate(
            [jnp.concatenate([low_h, low_l], axis=1), jnp.concatenate([high_h, high_l], axis=1)], axis=0
        )
        result = dot(hot, operand)
        result = result[:, :LANES] + result[:, LANES:]
        old = sums[...]
        put((before + (grid - 1)) & (grid - 1), transposed(old))
        moved = jnp.where(lane_y < HALF, pltpu.roll(old, HALF, 1), 0.0)
        sums[...] = result + jnp.where(row == before, old, moved)

    fetch(0, buffer_a)

    def pair(m, carry):
        fetch(2 * m + 1, buffer_b)
        work(2 * m, buffer_a)
        fetch(2 * m + 2, buffer_a)
        work(2 * m + 1, buffer_b)
        return carry

    lax.fori_loop(0, total_ref[0], pair, 0)
    last = sums[...]
    put(grid - 2, transposed(last))
    wrapped = transposed(pltpu.roll(last, HALF, 1))
    for side in range(grid // LANES):
        place = pl.ds(grid - 1, width, stride=grid)
        out_ref[side, place, :] = out_ref[side, place, :] + wrapped[:, side * LANES : (side + 1) * LANES]


def scatter_call(pairs, chunk_row, chunk_start, point, parts, images, weights, keys, cap, width, grid):
    sources, groups, rows16, _ = images.shape
    dirs = parts.shape[1]
    points = dirs * grid
    smem = pl.BlockSpec(memory_space=pltpu.SMEM)
    vmem = pl.BlockSpec(memory_space=VMEM)
    return pl.pallas_call(
        functools.partial(scatter_kernel, cap, width, grid),
        out_shape=jax.ShapeDtypeStruct((grid // LANES, width * grid, LANES), F32),
        in_specs=[smem] * 4 + [vmem] * 4,
        out_specs=vmem,
        scratch_shapes=[
            VMEM((points, LANES), F32),
            VMEM((CHUNK, LANES), F32),
            VMEM((CHUNK, LANES), F32),
            VMEM((grid, LANES), F32),
            VMEM((weights.shape[1], sources * rows16), BF16),
        ],
        compiler_params=pltpu.CompilerParams(vmem_limit_bytes=60 * 2**20),
        name="scatter",
    )(pairs, chunk_row, chunk_start, point, parts, images, weights, keys)


def plane_kernel(slabs, data_ref, yh_ref, yl_ref, xh_ref, xl_ref, out_ref, rows16):
    width, grid = data_ref.shape[1] // 2, data_ref.shape[2]
    half = grid // 2
    slab = grid // slabs
    lane = lax.broadcasted_iota(jnp.int32, (grid, half), 1)

    def one(z, carry):
        parts = []
        for r in range(2):
            plane = jnp.concatenate([data_ref[side, 2 * z + r] for side in range(grid // LANES)], axis=1)
            high, low = two_terms(plane)
            parts.append(dot(high, yh_ref[...]) + dot(low, yh_ref[...]) + dot(high, yl_ref[...]))
        cos_r, sin_r = parts[0][:, :half], parts[0][:, half:]
        cos_i, sin_i = parts[1][:, :half], parts[1][:, half:]
        zero_r = jnp.where(lane == 0, 0.0, sin_r)
        zero_i = jnp.where(lane == 0, 0.0, sin_i)
        real = jnp.concatenate([cos_r - zero_i, jnp.where(lane == 0, sin_r, cos_r + sin_i)], axis=1)
        imag = jnp.concatenate([cos_i + zero_r, jnp.where(lane == 0, sin_i, cos_i - sin_r)], axis=1)
        high, low = two_terms(jnp.concatenate([real, imag], axis=1))
        both = dot(xh_ref[...], high) + dot(xh_ref[...], low) + dot(xl_ref[...], high)
        rows = half + 8
        cos_r, cos_i = both[:rows, :grid], both[:rows, grid:]
        sin_r, sin_i = both[rows:, :grid], both[rows:, grid:]
        fields = ((cos_r - sin_i, cos_r + sin_i), (cos_i + sin_r, cos_i - sin_r))
        for c in range(2):
            plus, minus = fields[c]
            for side in range(grid // LANES):
                cut = slice(side * LANES, (side + 1) * LANES)
                place = 2 * z + c
                rows16[side, pl.ds(place, half, stride=2 * width), :] = plus[:half, cut]
                rows16[side, pl.ds(half * 2 * width + place, half, stride=2 * width), :] = minus[1 : half + 1, cut]
        return carry

    lax.fori_loop(0, width, one, 0)
    for d in range(slabs):
        if d < slabs // 2:
            start = slab * d
        else:
            start = half + grid - slab * d - slab
        size = slab * 2 * width
        for side in range(grid // LANES):
            block = rows16[side, start * 2 * width : start * 2 * width + size, :]
            out_ref[d, :, :, side * LANES : (side + 1) * LANES] = block.astype(BF16).reshape(slab, 2 * width, LANES)


def planes_call(data, table_y, table_x, slabs):
    sides, values, grid, _ = data.shape
    step = min(16, values)
    slab = grid // slabs
    fixed = lambda i: (0, 0)
    return pl.pallas_call(
        functools.partial(plane_kernel, slabs),
        grid=(values // step,),
        out_shape=jax.ShapeDtypeStruct((slabs, slab, values, grid), BF16),
        in_specs=[
            pl.BlockSpec((sides, step, grid, LANES), lambda i: (0, i, 0, 0)),
            pl.BlockSpec(table_y[0].shape, fixed),
            pl.BlockSpec(table_y[1].shape, fixed),
            pl.BlockSpec(table_x[0].shape, fixed),
            pl.BlockSpec(table_x[1].shape, fixed),
        ],
        out_specs=pl.BlockSpec((slabs, slab, step, grid), lambda i: (0, 0, i, 0)),
        scratch_shapes=[VMEM((sides, grid * step, LANES), F32)],
        compiler_params=pltpu.CompilerParams(vmem_limit_bytes=56 * 2**20),
        name="planes",
    )(data, *table_y, *table_x)


def volume_kernel(flip_ref, data_ref, restore_ref, zh_ref, zl_ref, out_ref):
    slabs, _, width, grid = data_ref.shape
    block = data_ref[...].reshape(slabs * width, grid)
    turned = dot_t(restore_ref[...], block).astype(BF16)
    out_ref[0] = dot(turned, zh_ref[...]) + dot(turned, zl_ref[...])


def volume_call(flip, data, restore, table_z):
    slabs, slab, width, grid = data.shape
    fixed = lambda i, flip_ref: (0, 0)
    return pl.pallas_call(
        volume_kernel,
        grid_spec=pltpu.PrefetchScalarGridSpec(
            num_scalar_prefetch=1,
            grid=(slab,),
            in_specs=[
                pl.BlockSpec((slabs, 1, width, grid), lambda i, flip_ref: (0, i, 0, 0)),
                pl.BlockSpec(restore.shape, fixed),
                pl.BlockSpec(table_z[0].shape, fixed),
                pl.BlockSpec(table_z[1].shape, fixed),
            ],
            out_specs=pl.BlockSpec(
                (1, grid, grid), lambda i, flip_ref: (jnp.where(flip_ref[0] == 1, slab - 1 - i, i), 0, 0)
            ),
        ),
        out_shape=jax.ShapeDtypeStruct((slab, grid, grid), F32),
        compiler_params=pltpu.CompilerParams(vmem_limit_bytes=48 * 2**20),
        name="volume",
    )(flip, data, restore, *table_z)


def sorted_points(interp_cells, grid):
    dirs = interp_cells.shape[0]
    points = dirs * grid
    base = interp_cells[:, 0, :].T.reshape(-1)
    row = (base // grid + 1) & (grid - 1)
    key = (row << 23) | ((base & (grid - 1)) << 15) | jnp.arange(points, dtype=jnp.int32)
    key = lax.sort(key, is_stable=False)
    rows = jnp.arange(grid, dtype=jnp.int32)
    count = jnp.sum((row[None, :] == rows[:, None]).astype(jnp.int32), axis=1)
    first = jnp.cumsum(count) - count
    chunks = jnp.maximum((count + (CHUNK - 1)) // CHUNK, 1)
    ends = jnp.cumsum(chunks)
    most = grid + points // CHUNK + 2
    number = jnp.arange(most, dtype=jnp.int32)
    chunk_row = jnp.minimum(jnp.sum((ends[None, :] <= number[:, None]).astype(jnp.int32), axis=1), grid - 1)
    mine = (rows[None, :] == chunk_row[:, None]).astype(jnp.int32)
    shift = first - (ends - chunks) * CHUNK
    chunk_start = jnp.sum(mine * shift[None, :], axis=1) + number * CHUNK
    chunk_start = jnp.where(number < ends[-1], chunk_start, points)
    pairs = ((ends[-1] + 1) // 2).reshape(1)
    point = jnp.concatenate([key & (points - 1), jnp.zeros((CHUNK,), jnp.int32)])
    keys = jnp.concatenate([key, jnp.full((8 * LANES,), -1, jnp.int32)]).reshape(-1, LANES)
    return pairs, chunk_row, chunk_start, point, keys


def shards(images, projections, assignment, interp_cells, interp_weights):
    class_count = lax.axis_size("cls")
    slab_count = lax.axis_size("vol")
    local_count, grid = images.shape[0], images.shape[1]
    dirs = projections.shape[1]
    slab = grid // slab_count
    width = 2 * slab
    halves = LANES // width
    capacity = 2 * local_count // class_count
    steps = 16 // capacity
    groups = grid // (halves * steps)

    classes = assignment[:, 0]
    onehot = (classes[:, None] == jnp.arange(class_count, dtype=jnp.int32)[None, :]).astype(jnp.int32)
    before = jnp.cumsum(onehot, axis=0) - onehot
    slot_index = classes * capacity + jnp.sum(before * onehot, axis=1)
    slot_table = jnp.full((class_count * capacity,), local_count, jnp.int32)
    slot_table = slot_table.at[slot_index].set(jnp.arange(local_count, dtype=jnp.int32))
    split = images.reshape(local_count, slab_count, slab, 2, halves, groups, steps)
    split = jnp.transpose(split, (0, 1, 5, 6, 4, 2, 3)).reshape(local_count, slab_count, groups, steps, LANES)
    outgoing = split.at[slot_table].get(mode="fill", fill_value=0)
    outgoing = outgoing.reshape(class_count, capacity, slab_count, groups, steps, LANES)
    outgoing = jnp.transpose(outgoing, (0, 2, 3, 4, 1, 5))
    outgoing = outgoing.reshape(class_count * slab_count, groups, steps * capacity, LANES)
    arrived = lax.all_to_all(outgoing, ("cls", "vol"), split_axis=0, concat_axis=0, tiled=True)

    references = projections[0].reshape(dirs, slab, 2, halves, groups, steps)
    references = jnp.transpose(references, (4, 5, 0, 3, 1, 2)).reshape(groups, steps * dirs, LANES)
    weights = interp_weights.reshape(dirs, 4, halves, groups, steps)
    weights = jnp.transpose(weights, (3, 4, 0, 2, 1)).reshape(groups, steps * dirs, 4 * halves)
    weights = jnp.pad(weights, ((0, 0), (0, 0), (0, LANES - 4 * halves)))
    pairs, chunk_row, chunk_start, point, keys = sorted_points(interp_cells, grid)
    table_y, table_x, table_z, restore = tables(grid, slab_count)

    partial_value = scores_call(arrived, references, capacity, dirs)
    copies = jnp.broadcast_to(partial_value[None], (slab_count,) + partial_value.shape)
    parts = lax.all_to_all(copies, "vol", split_axis=0, concat_axis=0, tiled=True)
    plane = scatter_call(
        pairs, chunk_row, chunk_start, point, parts, arrived, weights, keys, capacity, width, grid
    )
    plane = plane.reshape(grid // LANES, width, grid, LANES)
    sent = planes_call(plane, table_y, table_x, slab_count)
    received = lax.all_to_all(sent, "vol", split_axis=0, concat_axis=0, tiled=True)
    flip = (lax.axis_index("vol") >= slab_count // 2).astype(jnp.int32).reshape(1)
    return volume_call(flip, received, restore, table_z)[None]


def solution(mesh):
    in_specs = (
        P(("cls", "vol"), None, None, None),
        P("cls", None, "vol", None, None),
        P(("cls", "vol"), None),
        P(),
        P(),
    )
    out_specs = P("cls", "vol", None, None)
    return jax.shard_map(shards, mesh=mesh, in_specs=in_specs, out_specs=out_specs, check_vma=False)
```

time: 1420 us -> 520 us (0.37); the launches traced: 1400 us -> 518 us
  other arithmetic: 740 us -> 18.3 us
  Pallas kernels: 0 us -> 237 us
  matrix products: 145 us -> 0 us
  waiting for transfers between devices: 267 us -> 140 us
  local copies, waits for them, and re-layouts: 213 us -> 105 us
    scatter-add x1 -> x0, other arithmetic: 707 us -> none  [shards(): fourier_plane.at[interp_cells.reshape(-1)]]
    pallas_call x0 -> x4, Pallas kernels: none -> 237 us  [the longest x1 162 us: scatter_call(): pl.pallas_call(functools.partial(scatter_kernel, cap, width, grid), out_s...]
    dot_general x12 -> x0, matrix products: 145 us -> none  [the longest x1 20.2 us: shards(): jnp.einsum('zxy,zw->xyw', real_piece, cosine, precision=PRECISE)]
    mul x3 -> x0, local copies, waits for them, and re-layouts: 88.4 us -> none  [shards(): jnp.transpose(spread, (0, 3, 1, 2))[:, None, :, :, :]]
    all_to_all x3, waiting for transfers between devices: 222 us -> 140 us  [the longest x1 94.1 us: shards(): lax.all_to_all(sent, 'vol', split_axis=0, concat_axis=0, tiled=True)]
    psum x1 -> x0, waiting for transfers between devices: 44.8 us -> none  [shards(): scores = lax.psum(partial_value, 'vol')]
    transpose x0 -> x5, local copies, waits for them, and re-layouts: none -> 27.1 us  [the longest x1 14.7 us: shards(): jnp.transpose(split, (0, 1, 5, 6, 4, 2, 3))]
    scatter-add x1 -> x0, local copies, waits for them, and re-layouts: 24.5 us -> none  [shards(): fourier_plane.at[interp_cells.reshape(-1)]]
  transfers between devices with their start and end apart: 4 -> 3, of which waited for: 4 -> 3; matrix products, arithmetic and copies ran while one was open for 5% -> 11% of each run, Pallas kernels for 0% -> 0%
where the time goes in v1:
time: 520 us; the launch traced here: 518 us
  Pallas kernels  237 us (46%)
  waiting for transfers between devices  140 us (27%)
  local copies, waits for them, and re-layouts  105 us (20%)
  other arithmetic  18.3 us (4%)
  starting transfers between devices  16.3 us (3%)
    pallas_call x1, Pallas kernels, scatter_call(): pl.pallas_call(functools.partial(scatter_kernel, cap, width, grid), out_s...  162 us
    all_to_all x1, waiting for transfers between devices, shards(): lax.all_to_all(sent, 'vol', split_axis=0, concat_axis=0, tiled=True)  94.1 us
    all_to_all x1, waiting for transfers between devices, shards(): lax.all_to_all(outgoing, ('cls', 'vol'), split_axis=0, concat_axis=0, til...  38.1 us
    pallas_call x1, Pallas kernels, planes_call(): pl.pallas_call(functools.partial(plane_kernel, slabs), grid=(values // st...  34.5 us
    gather x2, local copies, waits for them, and re-layouts, shards(): outgoing = split.at[slot_table].get(mode='fill', fill_value=0)  27.9 us
    pallas_call x1, Pallas kernels, volume_call(): pl.pallas_call(volume_kernel, grid_spec=pltpu.PrefetchScalarGridSpec(num_...  26.8 us
    transpose x1, local copies, waits for them, and re-layouts, shards(): jnp.transpose(split, (0, 1, 5, 6, 4, 2, 3))  14.7 us
    unnamed x15, local copies, waits for them, and re-layouts  14.1 us
  transfers between devices with their start and end apart: 3, of which 3 were waited for; matrix products, arithmetic and copies ran while one was open for 11% of the time, Pallas kernels for 0%

profile of v1, /device:TPU:0, one launch (start us, length us, event | category | flops | bytes accessed | tf_op | source)
XLA Modules:
  0.0 517.5 jit_solution(13057334411237234153)
XLA Ops:
  0.0 0.7 fusion.8
  0.7 0.2 reduce_window_sum.51
  0.8 0.7 select_reduce_fusion.1
  1.5 0.7 fusion.11
  2.2 0.6 scatter_custom_fusion
  2.8 4.7 copy.29
  7.5 6.1 %reshape.169 = bf16[8,8,32,2,2,32,4]{2,1,6,5,4,3,0:T(8,128)(2,1)} reshape(bf16[8,256,2,256]{1,3,2,0:T(8,128)(2,1)S(1)} %copy.29) | data formatting | bytes 4194304 | tf_op jit(solution)/shard_map/reshape | solution.py:399
  13.6 14.7 %copy.30 = bf16[8,8,32,4,2,32,2]{2,1,6,5,4,3,0:T(8,128)(2,1)} copy(bf16[8,8,32,4,2,32,2]{5,1,3,2,4,6,0:T(8,128)(2,1)} %bitcast.74) | data formatting | bytes 4194304 | tf_op jit(solution)/shard_map/transpose | solution.py:400
  28.3 10.4 %gather_fusion = bf16[16,8,32,4,128]{2,1,4,3,0:T(8,128)(2,1)} fusion(bf16[8,8,32,4,128]{2,1,4,3,0:T(8,128)(2,1)} %bitcast.75, s32[1024]{0:T(1024)S(1)} %pad_clamp_fusion), kind=kCustom, calls=%fused_computation | custom fusion | bytes 8388672 | tf_op jit(solution)/shard_map/gather | solution.py:401
  38.7 17.5 %copy.31 = bf16[16,8,32,4,128]{4,2,3,1,0:T(8,128)(2,1)} copy(bf16[16,8,32,4,128]{2,1,4,3,0:T(8,128)(2,1)} %gather_fusion) | data formatting | bytes 8388608 | tf_op jit(solution)/shard_map/gather | solution.py:401
  56.2 0.1 broadcast_in_dim.17
  56.3 2.5 select_bitcast_fusion
  58.8 5.9 %copy.32 = bf16[4,8,32,4,4,128]{5,4,3,2,1,0:T(4,128)(2,1)} copy(bf16[4,8,32,4,4,128]{5,2,3,1,4,0:T(8,128)(2,1)S(1)} %select_bitcast_fusion) | data formatting | bytes 8388608 | tf_op jit(solution)/shard_map/transpose | solution.py:403
  64.7 7.6 %all-to-all-start = ((bf16[32,32,16,128]{3,2,1,0:T(8,128)(2,1)}), bf16[32,32,16,128]{3,2,1,0:T(8,128)(2,1)}, u32[]{:S(2)}, u32[]{:S(2)}) async-start(bf16[32,32,16,128]{3,2,1,0:T(8,128)(2,1)} %bitcast.77), calls=%async_computation | async-start | bytes 8388608 | tf_op jit(solution)/shard_map/all_to_all | solution.py:405
  72.3 0.1 copy.40
  72.4 0.1 fusion.6
  72.5 3.8 convert_reduce_fusion
  76.3 0.3 reduce-window.16
  76.8 0.3 reduce-window.24
  77.2 0.1 slice_reduce_fusion
  77.3 0.1 fusion.9
  77.4 0.6 slice.24
  78.6 8.4 %copy.33 = bf16[1,128,32,2,256]{1,2,4,3,0:T(8,128)(2,1)} copy(bf16[1,128,32,2,256]{4,3,2,1,0:T(2,128)(2,1)} %param.13) | data formatting | bytes 8388608 | tf_op args[1]
  86.9 6.3 %copy.34 = bf16[32,4,128,2,32,2]{2,1,5,4,3,0:T(4,128)(2,1)} copy(bf16[32,4,128,2,32,2]{2,4,1,0,3,5:T(8,128)(2,1)} %bitcast.78) | data formatting | bytes 8388608 | tf_op jit(solution)/shard_map/transpose | solution.py:408
  93.2 7.2 %reshape.172 = bf16[32,512,128]{1,2,0:T(8,128)(2,1)} reshape(bf16[32,4,128,2,32,2]{2,1,5,4,3,0:T(4,128)(2,1)} %copy.34) | data formatting | bytes 8388608 | tf_op jit(solution)/shard_map/reshape | solution.py:408
  100.4 6.5 %copy.35.refs_ref = bf16[32,512,128]{2,1,0:T(8,128)(2,1)} copy(bf16[32,512,128]{1,2,0:T(8,128)(2,1)} %reshape.172) | data formatting | bytes 8388608 | tf_op jit(solution)/shard_map/reshape | solution.py:408
  106.9 7.3 %sort.7 = s32[32768]{0:T(1024)S(1)} sort(s32[32768]{0:T(1024)S(1)} %get-tuple-element.7), dimensions={0}, to_apply=%region_7.8 | sort | flops 491520 | bytes 262144 | tf_op jit(solution)/shard_map/sort | solution.py:362
  114.2 0.7 concatenate.6.point_ref
  114.9 0.2 copy.36
  115.1 0.1 copy.37
  115.3 0.2 reshape.174
  115.5 4.8 copy.38
  120.3 7.5 %pad.6.weights_ref = f32[32,512,128]{2,1,0:T(8,128)} pad(f32[32,512,8]{2,1,0:T(8,128)} %copy.38, f32[]{:T(128)} %constant.101.clone.1), padding=0_0x0_0x0_120 | pad | bytes 8912900 | tf_op jit(solution)/shard_map/jit(_pad)/pad | solution.py:411
  127.8 0.2 convert_reduce_fusion.1
  128.0 38.1 %all-to-all-done.images_ref = bf16[32,32,16,128]{3,2,1,0:T(8,128)(2,1)} async-done(((bf16[32,32,16,128]{3,2,1,0:T(8,128)(2,1)}), bf16[32,32,16,128]{3,2,1,0:T(8,128)(2,1)}, u32[]{:S(2)}, u32[]{:S(2)}) %all-to-all-start) | async-done | bytes 4194336 | tf_op jit(solution)/shard_map/all_to_all | solution.py:405
  166.1 13.6 %scores.1 = f32[128,128]{1,0:T(8,128)S(1)} custom-call(bf16[32,32,16,128]{3,2,1,0:T(8,128)(2,1)} %all-to-all-done.images_ref, bf16[32,512,128]{2,1,0:T(8,128)(2,1)} %copy.35.refs_ref), custom_call_target="tpu_custom_call" | custom-call | tf_op jit(solution)/shard_map/scores/pallas_call | solution.py:89
  179.7 0.8 broadcast_in_dim.40
  180.6 3.6 all-to-all-start.1
  184.2 0.7 pad_bitcast_fusion.keys_ref
  184.8 0.3 select_reduce_fusion
  185.1 1.2 add_select_fusion.1.chunk_start_ref
  186.2 7.7 %all-to-all-done.1.parts_ref = f32[8,128,128]{2,1,0:T(8,128)S(1)} async-done(((f32[8,128,128]{2,1,0:T(8,128)}), f32[8,128,128]{2,1,0:T(8,128)S(1)}, u32[]{:S(2)}, u32[]{:S(2)}) %all-to-all-start.1) | async-done | bytes 524320 | tf_op jit(solution)/shard_map/all_to_all | solution.py:417
  193.9 0.8 copy-done.3
  194.7 162.3 %scatter.12 = f32[2,16384,128]{2,1,0:T(8,128)} custom-call(s32[1]{0:T(128)} %bitcast.7.total_ref, s32[514]{0:T(1024)} %copy-done.5, s32[514]{0:T(1024)} %add_select_fusion.1.chunk_start_ref, s32[32896]{0:T(1024)} %concatenate.6.point_ref, f32[8,128,128]{2,1,0:T(8,128)} %copy-done.3, bf16[32,32,16,128]{3,2,1,0:T(8,128)(2,1)} %all-to-all-done.images_ref, ...), custom_call_target="tpu_custom_call" | custom-call | tf_op jit(solution)/shard_map/scatter/pallas_call | solution.py:240
  357.0 34.5 %planes.1 = bf16[8,32,64,256]{3,2,1,0:T(8,128)(2,1)} custom-call(f32[2,64,256,128]{3,2,1,0:T(8,128)} %bitcast.73, bf16[256,256]{1,0:T(8,128)(2,1)} %constant.102.clone.yh_ref, bf16[256,256]{1,0:T(8,128)(2,1)} %constant.103.clone.yl_ref, bf16[272,256]{1,0:T(8,128)(2,1)} %constant.104.clone.xh_ref, bf16[272,256]{1,0:T(8,128)(2,1)} %constant.105.clone.xl_ref), custom_call_target="tpu_custom_call" | custom-call | tf_op jit(solution)/shard_map/planes/pallas_call | solution.py:307
  391.5 5.1 all-to-all-start.2
  396.6 94.1 %all-to-all-done.2.data_ref = bf16[8,32,64,256]{3,2,1,0:T(8,128)(2,1)} async-done(((bf16[8,32,64,256]{3,2,1,0:T(8,128)(2,1)}), bf16[8,32,64,256]{3,2,1,0:T(8,128)(2,1)}, u32[]{:S(2)}, u32[]{:S(2)}) %all-to-all-start.2) | async-done | bytes 8388640 | tf_op jit(solution)/shard_map/all_to_all | solution.py:423
  490.7 26.8 %volume.1 = f32[32,256,256]{2,1,0:T(8,128)} custom-call(s32[1]{0:T(128)} %bitcast.flip_ref, bf16[8,32,64,256]{3,2,1,0:T(8,128)(2,1)} %all-to-all-done.2.data_ref, bf16[256,256]{1,0:T(8,128)(2,1)S(1)} %copy-done.2, bf16[512,256]{1,0:T(8,128)(2,1)S(1)} %copy-done, bf16[512,256]{1,0:T(8,128)(2,1)S(1)} %copy-done.1), custom_call_target="tpu_custom_call" | custom-call | tf_op jit(solution)/shard_map/volume/pallas_call | solution.py:335
  (24 shorter events, 0.3 us)
Async XLA Ops:
  64.7 7.6 %slice-start = ((s32[128,4,256]{2,1,0:T(4,128)}), s32[128,1,256]{2,1,0:T(1,128)S(1)}, s32[]{:S(2)}) async-start(s32[128,4,256]{2,1,0:T(4,128)} %param.15), calls=%async_computation.3 | async-start | bytes 262144 | tf_op jit(solution)/shard_map/slice | solution.py:359
  64.7 101.4 %all-to-all-start = ((bf16[32,32,16,128]{3,2,1,0:T(8,128)(2,1)}), bf16[32,32,16,128]{3,2,1,0:T(8,128)(2,1)}, u32[]{:S(2)}, u32[]{:S(2)}) async-start(bf16[32,32,16,128]{3,2,1,0:T(8,128)(2,1)} %bitcast.77), calls=%async_computation | async-start | bytes 8388608 | tf_op jit(solution)/shard_map/all_to_all | solution.py:405
  100.4 14.5 %copy-start.4 = (f32[128,4,256]{2,1,0:T(4,128)S(1)}, f32[128,4,256]{2,1,0:T(4,128)}, u32[]{:S(2)}) copy-start(f32[128,4,256]{2,1,0:T(4,128)} %param.16) | copy-start | bytes 1572868
  128.0 56.8 %copy-start.5 = (s32[514]{0:T(1024)}, s32[514]{0:T(1024)S(1)}, u32[]{:S(2)}) copy-start(s32[514]{0:T(1024)S(1)} %broadcast_minimum_fusion.chunk_row_ref) | copy-start | bytes 6172
  180.6 13.3 %all-to-all-start.1 = ((f32[8,128,128]{2,1,0:T(8,128)}), f32[8,128,128]{2,1,0:T(8,128)S(1)}, u32[]{:S(2)}, u32[]{:S(2)}) async-start(f32[8,128,128]{2,1,0:T(8,128)} %broadcast_in_dim.40), calls=%async_computation.1 | async-start | bytes 1048576 | tf_op jit(solution)/shard_map/all_to_all | solution.py:417
  193.9 0.8 copy-start.3
  391.5 99.2 %copy-start = (bf16[512,256]{1,0:T(8,128)(2,1)S(1)}, bf16[512,256]{1,0:T(8,128)(2,1)}, u32[]{:S(2)}) copy-start(bf16[512,256]{1,0:T(8,128)(2,1)} %constant.107.clone.zh_ref) | copy-start | bytes 786436
  391.5 99.2 %copy-start.1 = (bf16[512,256]{1,0:T(8,128)(2,1)S(1)}, bf16[512,256]{1,0:T(8,128)(2,1)}, u32[]{:S(2)}) copy-start(bf16[512,256]{1,0:T(8,128)(2,1)} %constant.108.clone.zl_ref) | copy-start | bytes 786436
  391.5 99.2 %copy-start.2 = (bf16[256,256]{1,0:T(8,128)(2,1)S(1)}, bf16[256,256]{1,0:T(8,128)(2,1)}, u32[]{:S(2)}) copy-start(bf16[256,256]{1,0:T(8,128)(2,1)} %constant.106.clone.restore_ref) | copy-start | bytes 393220
  391.5 99.2 %all-to-all-start.2 = ((bf16[8,32,64,256]{3,2,1,0:T(8,128)(2,1)}), bf16[8,32,64,256]{3,2,1,0:T(8,128)(2,1)}, u32[]{:S(2)}, u32[]{:S(2)}) async-start(bf16[8,32,64,256]{3,2,1,0:T(8,128)(2,1)} %planes.1), calls=%async_computation.2 | async-start | bytes 16777216 | tf_op jit(solution)/shard_map/all_to_all | solution.py:423

commit v2 on v1

--- a/solution.py
+++ b/solution.py
@@ -58,6 +58,50 @@
     return high, low
 
 
+def route_kernel(cap, slabs, width, classes_ref, images_ref, eye_ref, order_ref, out_ref, lines):
+    count, _, _, grid = images_ref.shape
+    halves = LANES // width
+    piece = grid // halves
+    lane = lax.broadcasted_iota(jnp.int32, (piece, LANES), 1)
+    lines[...] = jnp.zeros_like(lines)
+
+    def place(p, carry):
+        own = classes_ref[p, 0]
+        rank = 0
+        for q in range(count):
+            rank = rank + jnp.where((classes_ref[q, 0] == own) & (q < p), 1, 0)
+        image = images_ref[p].reshape(-1, grid)
+        turned = dot(dot_t(eye_ref[...], image).astype(BF16), order_ref[...])
+        for w in range(slabs):
+            tile = w * width // LANES * LANES
+            block = jnp.zeros((piece, LANES), F32)
+            for h in range(halves):
+                part = turned[h * piece : (h + 1) * piece, tile : tile + LANES]
+                shift = (h * width - (w * width - tile)) % LANES
+                part = part if shift == 0 else pltpu.roll(part, shift, 1)
+                block = jnp.where((lane >= h * width) & (lane < (h + 1) * width), part, block)
+            lines[own * slabs + w, pl.ds(rank, piece, stride=cap), :] = block
+        return carry
+
+    lax.fori_loop(0, count, place, 0)
+    out_ref[...] = lines[...].astype(BF16).reshape(out_ref.shape)
+
+
+def route_call(images, assignment, eye, order, class_count, slabs, width, cap):
+    count, grid = images.shape[0], images.shape[1]
+    rows = grid // (LANES // width) * cap
+    vmem = pl.BlockSpec(memory_space=VMEM)
+    return pl.pallas_call(
+        functools.partial(route_kernel, cap, slabs, width),
+        out_shape=jax.ShapeDtypeStruct((class_count * slabs, rows // 16, 16, LANES), BF16),
+        in_specs=[pl.BlockSpec(memory_space=pltpu.SMEM)] + [vmem] * 3,
+        out_specs=vmem,
+        scratch_shapes=[VMEM((class_count * slabs, rows, LANES), F32)],
+        compiler_params=pltpu.CompilerParams(vmem_limit_bytes=48 * 2**20),
+        name="route",
+    )(assignment, images, eye, order)
+
+
 def score_kernel(cap, dirs, images_ref, refs_ref, out_ref, sums):
     sources, groups, rows16, _ = images_ref.shape
     rows = sources * rows16
@@ -65,11 +109,12 @@
     sums[...] = jnp.zeros_like(sums)
 
     def step(g, carry):
-        block = images_ref[:, pl.ds(g, 1), :, :].reshape(rows, LANES)
-        sums[...] += dot_t(refs_ref[g], block)
+        blocks = [images_ref[:, pl.ds(2 * g + i, 1), :, :].reshape(rows, LANES) for i in range(2)]
+        refs = [refs_ref[2 * g + i] for i in range(2)]
+        sums[...] += dot_t(jnp.concatenate(refs, axis=1), jnp.concatenate(blocks, axis=1))
         return carry
 
-    lax.fori_loop(0, groups, step, 0)
+    lax.fori_loop(0, groups // 2, step, 0)
     column = lax.broadcasted_iota(jnp.int32, (dirs, rows), 1)
     part = (column & (rows16 - 1)) // cap
     kept = jnp.zeros((dirs, rows), F32)
@@ -104,11 +149,11 @@
     total_ref,
     chunk_row_ref,
     chunk_start_ref,
+    chunk_size_ref,
     point_ref,
     parts_ref,
     images_ref,
     weights_ref,
-    keys_ref,
     out_ref,
     values,
     buffer_a,
@@ -144,7 +189,7 @@
         weight = weights_ref[g]
         for h in range(halves):
             shifted = mean if h == 0 else pltpu.roll(mean, LANES - h * width, 1)
-            behind = pltpu.roll(weight, HALF - 4 * h, 1)
+            behind = pltpu.roll(weight, HALF - 8 * h, 1)
             start = pl.multiple_of((h * groups + g) * joined, joined)
             values[pl.ds(start, joined), :] = jnp.where(lane_j < HALF, shifted, behind)
         return carry
@@ -155,63 +200,48 @@
     buffer_b[...] = jnp.zeros_like(buffer_b)
     sums[...] = jnp.zeros_like(sums)
 
-    lane = lax.broadcasted_iota(jnp.int32, (CHUNK, LANES), 1)
-    lane_y = lax.broadcasted_iota(jnp.int32, (grid, LANES), 1)
-    cell_y = lax.broadcasted_iota(jnp.int32, (grid, CHUNK), 0)
-    lane_8 = lax.broadcasted_iota(jnp.int32, (8, LANES), 1)
-    pick_row = lax.broadcasted_iota(jnp.int32, (width, LANES), 0)
-    pick_lane = lax.broadcasted_iota(jnp.int32, (width, LANES), 1)
-    pick = ((pick_lane == pick_row) | (pick_lane == pick_row + HALF)).astype(F32).astype(BF16)
+    place = lax.broadcasted_iota(jnp.int32, (CHUNK, LANES), 0)
+    lane = lax.broadcasted_iota(jnp.int32, (CHUNK, grid), 1)
+    at_y = lane.astype(F32).astype(BF16)
+    at_next = ((lane + (grid - 1)) & (grid - 1)).astype(F32).astype(BF16)
+    one = jnp.ones((CHUNK, grid), BF16)
+    none = jnp.zeros((CHUNK, grid), BF16)
 
     def fetch(c, buffer):
         start = chunk_start_ref[c]
         for i in range(CHUNK):
             buffer[pl.ds(i, 1), :] = values[pl.ds(point_ref[start + i], 1), :]
 
-    def transposed(plane):
-        high = plane.astype(BF16).astype(F32)
-        both = jnp.where(lane_y < HALF, high, pltpu.roll(plane - high, HALF, 1)).astype(BF16)
-        return dot_t(pick, both)
-
-    def put(x, flipped):
+    def put(x, plane):
         for side in range(grid // LANES):
-            out_ref[side, pl.ds(x, width, stride=grid), :] = flipped[:, side * LANES : (side + 1) * LANES]
+            out_ref[side, pl.ds(x, width, stride=grid), :] = plane[:, side * LANES : (side + 1) * LANES]
 
     def work(c, buffer):
         row = chunk_row_ref[c]
         before = chunk_row_ref[jnp.maximum(c - 1, 0)]
-        start = chunk_start_ref[c]
-        base = start >> 7
-        offset = start & (LANES - 1)
-        turn = LANES - offset
-        first = pltpu.roll(jnp.broadcast_to(keys_ref[pl.ds(base, 1), :], (8, LANES)), turn, 1)
-        second = pltpu.roll(jnp.broadcast_to(keys_ref[pl.ds(base + 1, 1), :], (8, LANES)), turn, 1)
-        key = jnp.where(lane_8 < turn, first, second)
-        valid = (key >> 23) == row
-        y = (key >> 15) & (grid - 1)
-        low_y = jnp.where(valid, y, -1)[0:1, :]
-        high_y = jnp.where(valid, (y + 1) & (grid - 1), -1)[0:1, :]
-        hot = jnp.concatenate(
+        data = buffer[...]
+        y = jnp.broadcast_to(data[:, HALF + 4 : HALF + 5], (CHUNK, LANES))
+        y = jnp.where(place < chunk_size_ref[c], y, -1.0).astype(BF16)
+        y = jnp.concatenate([y] * (grid // LANES), axis=1)
+        hot = jnp.concatenate([jnp.where(at_y == y, one, none), jnp.where(at_next == y, one, none)], axis=0)
+        turned = data.T
+        mean = turned[:width]
+        weight = [jnp.broadcast_to(turned[HALF + j : HALF + j + 1], (width, CHUNK)) for j in range(4)]
+        operand = jnp.concatenate(
             [
-                jnp.where(cell_y == low_y, 1.0, 0.0).astype(BF16),
-                jnp.where(cell_y == high_y, 1.0, 0.0).astype(BF16),
+                jnp.concatenate([mean * weight[0], mean * weight[2]], axis=1),
+                jnp.concatenate([mean * weight[1], mean * weight[3]], axis=1),
             ],
-            axis=1,
+            axis=0,
         )
-        data = buffer[...]
-        twice = jnp.where(lane < HALF, data, pltpu.roll(data, HALF, 1))
-        weight = [jnp.broadcast_to(data[:, HALF + j : HALF + j + 1], (CHUNK, LANES)) for j in range(4)]
-        low_h, low_l = two_terms(twice * jnp.where(lane < HALF, weight[0], weight[1]))
-        high_h, high_l = two_terms(twice * jnp.where(lane < HALF, weight[2], weight[3]))
-        operand = jnp.concatenate(
-            [jnp.concatenate([low_h, low_l], axis=1), jnp.concatenate([high_h, high_l], axis=1)], axis=0
-        )
-        result = dot(hot, operand)
-        result = result[:, :LANES] + result[:, LANES:]
-        old = sums[...]
-        put((before + (grid - 1)) & (grid - 1), transposed(old))
-        moved = jnp.where(lane_y < HALF, pltpu.roll(old, HALF, 1), 0.0)
-        sums[...] = result + jnp.where(row == before, old, moved)
+        high, low = two_terms(operand)
+        result = dot(jnp.concatenate([high, low], axis=0), hot)
+        result = result[: 2 * width] + result[2 * width :]
+        same = row == before
+        old_low, old_high = sums[:width], sums[width:]
+        put((before + (grid - 1)) & (grid - 1), old_low)
+        sums[:width] = result[:width] + jnp.where(same, old_low, old_high)
+        sums[width:] = result[width:] + jnp.where(same, old_high, 0.0)
 
     fetch(0, buffer_a)
 
@@ -223,15 +253,14 @@
         return carry
 
     lax.fori_loop(0, total_ref[0], pair, 0)
-    last = sums[...]
-    put(grid - 2, transposed(last))
-    wrapped = transposed(pltpu.roll(last, HALF, 1))
+    put(grid - 2, sums[:width])
     for side in range(grid // LANES):
-        place = pl.ds(grid - 1, width, stride=grid)
-        out_ref[side, place, :] = out_ref[side, place, :] + wrapped[:, side * LANES : (side + 1) * LANES]
-
-
-def scatter_call(pairs, chunk_row, chunk_start, point, parts, images, weights, keys, cap, width, grid):
+        wrapped = pl.ds(grid - 1, width, stride=grid)
+        cut = slice(side * LANES, (side + 1) * LANES)
+        out_ref[side, wrapped, :] = out_ref[side, wrapped, :] + sums[width:, cut]
+
+
+def scatter_call(plan, parts, images, weights, cap, width, grid):
     sources, groups, rows16, _ = images.shape
     dirs = parts.shape[1]
     points = dirs * grid
@@ -240,18 +269,18 @@
     return pl.pallas_call(
         functools.partial(scatter_kernel, cap, width, grid),
         out_shape=jax.ShapeDtypeStruct((grid // LANES, width * grid, LANES), F32),
-        in_specs=[smem] * 4 + [vmem] * 4,
+        in_specs=[smem] * 5 + [vmem] * 3,
         out_specs=vmem,
         scratch_shapes=[
             VMEM((points, LANES), F32),
             VMEM((CHUNK, LANES), F32),
             VMEM((CHUNK, LANES), F32),
-            VMEM((grid, LANES), F32),
+            VMEM((2 * width, grid), F32),
             VMEM((weights.shape[1], sources * rows16), BF16),
         ],
         compiler_params=pltpu.CompilerParams(vmem_limit_bytes=60 * 2**20),
         name="scatter",
-    )(pairs, chunk_row, chunk_start, point, parts, images, weights, keys)
+    )(*plan, parts, images, weights)
 
 
 def plane_kernel(slabs, data_ref, yh_ref, yl_ref, xh_ref, xl_ref, out_ref, rows16):
@@ -323,28 +352,32 @@
 
 
 def volume_kernel(flip_ref, data_ref, restore_ref, zh_ref, zl_ref, out_ref):
-    slabs, _, width, grid = data_ref.shape
-    block = data_ref[...].reshape(slabs * width, grid)
-    turned = dot_t(restore_ref[...], block).astype(BF16)
-    out_ref[0] = dot(turned, zh_ref[...]) + dot(turned, zl_ref[...])
+    slabs, span, width, grid = data_ref.shape
+    for i in range(span):
+        block = data_ref[:, i].reshape(slabs * width, grid)
+        turned = dot_t(restore_ref[...], block).astype(BF16)
+        value = dot(turned, zh_ref[...]) + dot(turned, zl_ref[...])
+        out_ref[jnp.where(flip_ref[0] == 1, span - 1 - i, i)] = value
 
 
 def volume_call(flip, data, restore, table_z):
     slabs, slab, width, grid = data.shape
+    span = 4
+    steps = slab // span
     fixed = lambda i, flip_ref: (0, 0)
     return pl.pallas_call(
         volume_kernel,
         grid_spec=pltpu.PrefetchScalarGridSpec(
             num_scalar_prefetch=1,
-            grid=(slab,),
+            grid=(steps,),
             in_specs=[
-                pl.BlockSpec((slabs, 1, width, grid), lambda i, flip_ref: (0, i, 0, 0)),
+                pl.BlockSpec((slabs, span, width, grid), lambda i, flip_ref: (0, i, 0, 0)),
                 pl.BlockSpec(restore.shape, fixed),
                 pl.BlockSpec(table_z[0].shape, fixed),
                 pl.BlockSpec(table_z[1].shape, fixed),
             ],
             out_specs=pl.BlockSpec(
-                (1, grid, grid), lambda i, flip_ref: (jnp.where(flip_ref[0] == 1, slab - 1 - i, i), 0, 0)
+                (span, grid, grid), lambda i, flip_ref: (jnp.where(flip_ref[0] == 1, steps - 1 - i, i), 0, 0)
             ),
         ),
         out_shape=jax.ShapeDtypeStruct((slab, grid, grid), F32),
@@ -358,7 +391,7 @@
     points = dirs * grid
     base = interp_cells[:, 0, :].T.reshape(-1)
     row = (base // grid + 1) & (grid - 1)
-    key = (row << 23) | ((base & (grid - 1)) << 15) | jnp.arange(points, dtype=jnp.int32)
+    key = row * points + jnp.arange(points, dtype=jnp.int32)
     key = lax.sort(key, is_stable=False)
     rows = jnp.arange(grid, dtype=jnp.int32)
     count = jnp.sum((row[None, :] == rows[:, None]).astype(jnp.int32), axis=1)
@@ -371,11 +404,13 @@
     mine = (rows[None, :] == chunk_row[:, None]).astype(jnp.int32)
     shift = first - (ends - chunks) * CHUNK
     chunk_start = jnp.sum(mine * shift[None, :], axis=1) + number * CHUNK
-    chunk_start = jnp.where(number < ends[-1], chunk_start, points)
+    row_end = jnp.sum(mine * (first + count)[None, :], axis=1)
+    used = number < ends[-1]
+    chunk_size = jnp.where(used, jnp.clip(row_end - chunk_start, 0, CHUNK), 0)
+    chunk_start = jnp.where(used, chunk_start, points)
     pairs = ((ends[-1] + 1) // 2).reshape(1)
     point = jnp.concatenate([key & (points - 1), jnp.zeros((CHUNK,), jnp.int32)])
-    keys = jnp.concatenate([key, jnp.full((8 * LANES,), -1, jnp.int32)]).reshape(-1, LANES)
-    return pairs, chunk_row, chunk_start, point, keys
+    return pairs, chunk_row, chunk_start, chunk_size, point
 
 
 def shards(images, projections, assignment, interp_cells, interp_weights):
@@ -390,34 +425,25 @@
     steps = 16 // capacity
     groups = grid // (halves * steps)
 
-    classes = assignment[:, 0]
-    onehot = (classes[:, None] == jnp.arange(class_count, dtype=jnp.int32)[None, :]).astype(jnp.int32)
-    before = jnp.cumsum(onehot, axis=0) - onehot
-    slot_index = classes * capacity + jnp.sum(before * onehot, axis=1)
-    slot_table = jnp.full((class_count * capacity,), local_count, jnp.int32)
-    slot_table = slot_table.at[slot_index].set(jnp.arange(local_count, dtype=jnp.int32))
-    split = images.reshape(local_count, slab_count, slab, 2, halves, groups, steps)
-    split = jnp.transpose(split, (0, 1, 5, 6, 4, 2, 3)).reshape(local_count, slab_count, groups, steps, LANES)
-    outgoing = split.at[slot_table].get(mode="fill", fill_value=0)
-    outgoing = outgoing.reshape(class_count, capacity, slab_count, groups, steps, LANES)
-    outgoing = jnp.transpose(outgoing, (0, 2, 3, 4, 1, 5))
-    outgoing = outgoing.reshape(class_count * slab_count, groups, steps * capacity, LANES)
+    eye = jnp.asarray(np.eye(grid), BF16)
+    order = jnp.asarray(np.eye(2 * grid), BF16)
+    outgoing = route_call(images, assignment, eye, order, class_count, slab_count, width, capacity)
     arrived = lax.all_to_all(outgoing, ("cls", "vol"), split_axis=0, concat_axis=0, tiled=True)
 
     references = projections[0].reshape(dirs, slab, 2, halves, groups, steps)
     references = jnp.transpose(references, (4, 5, 0, 3, 1, 2)).reshape(groups, steps * dirs, LANES)
-    weights = interp_weights.reshape(dirs, 4, halves, groups, steps)
-    weights = jnp.transpose(weights, (3, 4, 0, 2, 1)).reshape(groups, steps * dirs, 4 * halves)
-    weights = jnp.pad(weights, ((0, 0), (0, 0), (0, LANES - 4 * halves)))
-    pairs, chunk_row, chunk_start, point, keys = sorted_points(interp_cells, grid)
+    corner_y = (interp_cells[:, 0:1, :] & (grid - 1)).astype(F32)
+    weights = jnp.concatenate([interp_weights, corner_y, jnp.zeros((dirs, 3, grid), F32)], axis=1)
+    weights = weights.reshape(dirs, 8, halves, groups, steps)
+    weights = jnp.transpose(weights, (3, 4, 0, 2, 1)).reshape(groups, steps * dirs, 8 * halves)
+    weights = jnp.pad(weights, ((0, 0), (0, 0), (0, LANES - 8 * halves)))
+    plan = sorted_points(interp_cells, grid)
     table_y, table_x, table_z, restore = tables(grid, slab_count)
 
     partial_value = scores_call(arrived, references, capacity, dirs)
     copies = jnp.broadcast_to(partial_value[None], (slab_count,) + partial_value.shape)
     parts = lax.all_to_all(copies, "vol", split_axis=0, concat_axis=0, tiled=True)
-    plane = scatter_call(
-        pairs, chunk_row, chunk_start, point, parts, arrived, weights, keys, capacity, width, grid
-    )
+    plane = scatter_call(plan, parts, arrived, weights, capacity, width, grid)
     plane = plane.reshape(grid // LANES, width, grid, LANES)
     sent = planes_call(plane, table_y, table_x, slab_count)
     received = lax.all_to_all(sent, "vol", split_axis=0, concat_axis=0, tiled=True)

time: 520 us -> 425 us (0.82)
  local copies, waits for them, and re-layouts: 105 us -> 50.5 us
  Pallas kernels: 237 us -> 194 us
    pallas_call x1, Pallas kernels: 162 us -> 129 us  [scatter_call(): pl.pallas_call(functools.partial(scatter_kernel, cap, width, grid), out_s...]
    gather x2 -> x0, local copies, waits for them, and re-layouts: 27.9 us -> none  [shards(): outgoing = split.at[slot_table].get(mode='fill', fill_value=0)]
    transpose x2 -> x0, local copies, waits for them, and re-layouts: 20.6 us -> none  [the longest x1 14.7 us: shards(): jnp.transpose(split, (0, 1, 5, 6, 4, 2, 3))]
    pallas_call x1, Pallas kernels: 26.8 us -> 12.4 us  [volume_call(): pl.pallas_call(volume_kernel, grid_spec=pltpu.PrefetchScalarGridSpec(num_...]
    all_to_all x1, waiting for transfers between devices: 38.1 us -> 51 us  [shards(): lax.all_to_all(outgoing, ('cls', 'vol'), split_axis=0, concat_axis=0, til...]
    pallas_call x0 -> x1, Pallas kernels: none -> 8.34 us  [route_call(): pl.pallas_call(functools.partial(route_kernel, cap, slabs, width), out_sh...]
    all_to_all x1, waiting for transfers between devices: 7.66 us -> 0.01 us  [shards(): lax.all_to_all(copies, 'vol', split_axis=0, concat_axis=0, tiled=True)]
    reshape x2 -> x0, local copies, waits for them, and re-layouts: 6.75 us -> none  [the longest x1 6.09 us: shards(): images.reshape(local_count, slab_count, slab, 2, halves, groups, steps)]
  transfers between devices with their start and end apart: 3 -> 3, of which waited for: 3 -> 2; matrix products, arithmetic and copies ran while one was open for 11% -> 14% of each run, Pallas kernels for 0% -> 0%
where the time goes in v2:
time: 425 us; the launch traced here: 420 us
  Pallas kernels  194 us (46%)
  waiting for transfers between devices  145 us (34%)
  local copies, waits for them, and re-layouts  50.5 us (12%)
  starting transfers between devices  16.2 us (4%)
  other arithmetic  14 us (3%)
    pallas_call x1, Pallas kernels, scatter_call(): pl.pallas_call(functools.partial(scatter_kernel, cap, width, grid), out_s...  129 us
    all_to_all x1, waiting for transfers between devices, shards(): lax.all_to_all(sent, 'vol', split_axis=0, concat_axis=0, tiled=True)  94.1 us
    all_to_all x1, waiting for transfers between devices, shards(): lax.all_to_all(outgoing, ('cls', 'vol'), split_axis=0, concat_axis=0, til...  51 us
    pallas_call x1, Pallas kernels, planes_call(): pl.pallas_call(functools.partial(plane_kernel, slabs), grid=(values // st...  34.5 us
    unnamed x21, local copies, waits for them, and re-layouts  13.8 us
    reshape x2, local copies, waits for them, and re-layouts, shards(): jnp.transpose(references, (4, 5, 0, 3, 1, 2))  13.7 us
    pallas_call x1, Pallas kernels, volume_call(): pl.pallas_call(volume_kernel, grid_spec=pltpu.PrefetchScalarGridSpec(num_...  12.4 us
    pallas_call x1, Pallas kernels, scores_call(): pl.pallas_call(functools.partial(score_kernel, cap, dirs), out_shape=jax....  9.31 us
  transfers between devices with their start and end apart: 3, of which 2 were waited for; matrix products, arithmetic and copies ran while one was open for 14% of the time, Pallas kernels for 0%

profile of v2, /device:TPU:0, one launch (start us, length us, event | category | flops | bytes accessed | tf_op | source)
XLA Modules:
  0.0 420.2 jit_solution(13079875152141746802)
XLA Ops:
  0.0 0.7 copy.30.classes_ref
  0.7 1.6 copy-done
  2.3 1.0 copy-done.1
  3.4 0.9 copy-done.5
  4.3 8.3 %route.1 = bf16[32,32,16,128]{3,2,1,0:T(8,128)(2,1)} custom-call(s32[8,1]{1,0:T(8,128)S(1)} %copy.30.classes_ref, bf16[8,256,2,256]{3,2,1,0:T(2,128)(2,1)S(1)} %copy-done, bf16[256,256]{1,0:T(8,128)(2,1)S(1)} %copy-done.5, bf16[512,512]{1,0:T(8,128)(2,1)S(1)} %copy-done.1), custom_call_target="tpu_custom_call" | custom-call | tf_op jit(solution)/shard_map/route/pallas_call | solution.py:94
  12.6 7.4 %all-to-all-start = ((bf16[32,32,16,128]{3,2,1,0:T(8,128)(2,1)}), bf16[32,32,16,128]{3,2,1,0:T(8,128)(2,1)}, u32[]{:S(2)}, u32[]{:S(2)}) async-start(bf16[32,32,16,128]{3,2,1,0:T(8,128)(2,1)} %route.1), calls=%async_computation | async-start | bytes 8388608 | tf_op jit(solution)/shard_map/all_to_all | solution.py:431
  20.0 1.1 slice.22
  21.2 0.1 copy.39
  21.3 0.1 iota_add_fusion
  21.4 3.8 convert_reduce_fusion
  25.2 0.3 reduce-window.16
  25.5 0.1 slice.23
  25.6 0.3 reduce-window.24
  25.9 0.1 slice.26
  26.0 7.3 %sort.7 = s32[32768]{0:T(1024)S(1)} sort(s32[32768]{0:T(1024)S(1)} %get-tuple-element.7), dimensions={0}, to_apply=%region_8.9 | sort | flops 491520 | bytes 262144 | tf_op jit(solution)/shard_map/sort | solution.py:395
  33.3 8.5 %copy.31 = bf16[1,128,32,2,256]{1,2,4,3,0:T(8,128)(2,1)} copy(bf16[1,128,32,2,256]{4,3,2,1,0:T(2,128)(2,1)} %param.15) | data formatting | bytes 8388608 | tf_op args[1]
  41.8 6.3 %copy.32 = bf16[32,4,128,2,32,2]{2,1,5,4,3,0:T(4,128)(2,1)} copy(bf16[32,4,128,2,32,2]{2,4,1,0,3,5:T(8,128)(2,1)} %bitcast.46) | data formatting | bytes 8388608 | tf_op jit(solution)/shard_map/transpose | solution.py:434
  48.1 7.3 %reshape.156 = bf16[32,512,128]{1,2,0:T(8,128)(2,1)} reshape(bf16[32,4,128,2,32,2]{2,1,5,4,3,0:T(4,128)(2,1)} %copy.32) | data formatting | bytes 8388608 | tf_op jit(solution)/shard_map/reshape | solution.py:434
  55.3 6.4 %copy.33.refs_ref = bf16[32,512,128]{2,1,0:T(8,128)(2,1)} copy(bf16[32,512,128]{1,2,0:T(8,128)(2,1)} %reshape.156) | data formatting | bytes 8388608 | tf_op jit(solution)/shard_map/reshape | solution.py:434
  61.8 0.1 copy.35
  61.9 0.3 copy.34
  62.2 0.1 pad.8.clone
  62.2 0.1 slice_reduce_fusion
  62.4 0.1 multiply_subtract_fusion
  62.5 0.2 convert_reduce_fusion.1
  62.6 0.2 maximum_maximum_fusion
  62.9 51.0 %all-to-all-done.images_ref = bf16[32,32,16,128]{3,2,1,0:T(8,128)(2,1)} async-done(((bf16[32,32,16,128]{3,2,1,0:T(8,128)(2,1)}), bf16[32,32,16,128]{3,2,1,0:T(8,128)(2,1)}, u32[]{:S(2)}, u32[]{:S(2)}) %all-to-all-start) | async-done | bytes 4194336 | tf_op jit(solution)/shard_map/all_to_all | solution.py:431
  113.9 9.3 %scores.1 = f32[128,128]{1,0:T(8,128)S(1)} custom-call(bf16[32,32,16,128]{3,2,1,0:T(8,128)(2,1)} %all-to-all-done.images_ref, bf16[32,512,128]{2,1,0:T(8,128)(2,1)} %copy.33.refs_ref), custom_call_target="tpu_custom_call" | custom-call | tf_op jit(solution)/shard_map/scores/pallas_call | solution.py:134
  123.2 0.8 broadcast_in_dim.12
  124.0 3.7 all-to-all-start.1
  127.7 0.0 copy-start.8
  127.7 0.7 slice.25
  129.1 0.7 concatenate.6.point_ref
  129.8 0.3 copy.36
  130.1 0.4 reshape.158
  130.5 4.6 %copy.37 = f32[32,512,16]{2,1,0:T(8,128)} copy(f32[32,512,16]{1,2,0:T(8,128)S(1)} %reshape.158) | data formatting | bytes 2097152 | tf_op jit(solution)/shard_map/reshape | solution.py:438
  135.1 7.5 %pad.5.weights_ref = f32[32,512,128]{2,1,0:T(8,128)} pad(f32[32,512,16]{2,1,0:T(8,128)} %copy.37, f32[]{:T(128)} %constant.89.clone.1), padding=0_0x0_0x0_112 | pad | bytes 9437188 | tf_op jit(solution)/shard_map/jit(_pad)/pad | solution.py:439
  142.7 0.3 select_reduce_fusion
  143.1 1.3 clamp_select_fusion
  144.3 0.0 all-to-all-done.1.parts_ref
  144.4 0.8 copy-done.6
  145.1 129.0 %scatter.1 = f32[2,16384,128]{2,1,0:T(8,128)} custom-call(s32[1]{0:T(128)} %bitcast.7.total_ref, s32[514]{0:T(1024)} %copy-done.8, s32[514]{0:T(1024)} %get-tuple-element.13.chunk_start_ref, s32[514]{0:T(1024)} %get-tuple-element.12.chunk_size_ref, s32[32896]{0:T(1024)} %concatenate.6.point_ref, f32[8,128,128]{2,1,0:T(8,128)} %copy-done.6, ...), custom_call_target="tpu_custom_call" | custom-call | tf_op jit(solution)/shard_map/scatter/pallas_call | solution.py:269
  274.1 34.5 %planes.1 = bf16[8,32,64,256]{3,2,1,0:T(8,128)(2,1)} custom-call(f32[2,64,256,128]{3,2,1,0:T(8,128)} %bitcast.45, bf16[256,256]{1,0:T(8,128)(2,1)} %constant.92.clone.yh_ref, bf16[256,256]{1,0:T(8,128)(2,1)} %constant.93.clone.yl_ref, bf16[272,256]{1,0:T(8,128)(2,1)} %constant.94.clone.xh_ref, bf16[272,256]{1,0:T(8,128)(2,1)} %constant.95.clone.xl_ref), custom_call_target="tpu_custom_call" | custom-call | tf_op jit(solution)/shard_map/planes/pallas_call | solution.py:336
  308.6 5.1 %all-to-all-start.2 = ((bf16[8,32,64,256]{3,2,1,0:T(8,128)(2,1)}), bf16[8,32,64,256]{3,2,1,0:T(8,128)(2,1)}, u32[]{:S(2)}, u32[]{:S(2)}) async-start(bf16[8,32,64,256]{3,2,1,0:T(8,128)(2,1)} %planes.1), calls=%async_computation.2 | async-start | bytes 16777216 | tf_op jit(solution)/shard_map/all_to_all | solution.py:449
  313.7 94.1 %all-to-all-done.2.data_ref = bf16[8,32,64,256]{3,2,1,0:T(8,128)(2,1)} async-done(((bf16[8,32,64,256]{3,2,1,0:T(8,128)(2,1)}), bf16[8,32,64,256]{3,2,1,0:T(8,128)(2,1)}, u32[]{:S(2)}, u32[]{:S(2)}) %all-to-all-start.2) | async-done | bytes 8388640 | tf_op jit(solution)/shard_map/all_to_all | solution.py:449
  407.8 0.0 copy-done.2
  407.8 0.0 copy-done.4
  407.8 12.4 %volume.1 = f32[32,256,256]{2,1,0:T(8,128)} custom-call(s32[1]{0:T(128)} %bitcast.flip_ref, bf16[8,32,64,256]{3,2,1,0:T(8,128)(2,1)} %all-to-all-done.2.data_ref, bf16[256,256]{1,0:T(8,128)(2,1)S(1)} %copy-done.4, bf16[512,256]{1,0:T(8,128)(2,1)S(1)} %copy-done.2, bf16[512,256]{1,0:T(8,128)(2,1)S(1)} %copy-done.3), custom_call_target="tpu_custom_call" | custom-call | tf_op jit(solution)/shard_map/volume/pallas_call | solution.py:368
  (18 shorter events, 0.1 us)
Async XLA Ops:
  0.7 1.6 copy-start
  2.3 1.0 copy-start.1
  3.4 0.9 copy-start.5
  12.6 101.3 %all-to-all-start = ((bf16[32,32,16,128]{3,2,1,0:T(8,128)(2,1)}), bf16[32,32,16,128]{3,2,1,0:T(8,128)(2,1)}, u32[]{:S(2)}, u32[]{:S(2)}) async-start(bf16[32,32,16,128]{3,2,1,0:T(8,128)(2,1)} %route.1), calls=%async_computation | async-start | bytes 8388608 | tf_op jit(solution)/shard_map/all_to_all | solution.py:431
  48.1 13.8 %copy-start.7 = (f32[128,4,256]{2,1,0:T(4,128)S(1)}, f32[128,4,256]{2,1,0:T(4,128)}, u32[]{:S(2)}) copy-start(f32[128,4,256]{2,1,0:T(4,128)} %param.18) | copy-start | bytes 1572868
  124.0 20.3 %all-to-all-start.1 = ((f32[8,128,128]{2,1,0:T(8,128)}), f32[8,128,128]{2,1,0:T(8,128)S(1)}, u32[]{:S(2)}, u32[]{:S(2)}) async-start(f32[8,128,128]{2,1,0:T(8,128)} %broadcast_in_dim.12), calls=%async_computation.1 | async-start | bytes 1048576 | tf_op jit(solution)/shard_map/all_to_all | solution.py:445
  127.7 15.0 %copy-start.8 = (s32[514]{0:T(1024)}, s32[514]{0:T(1024)S(1)}, u32[]{:S(2)}) copy-start(s32[514]{0:T(1024)S(1)} %broadcast_minimum_fusion.chunk_row_ref) | copy-start | bytes 6172
  144.3 0.8 copy-start.6
  308.6 99.2 %copy-start.2 = (bf16[512,256]{1,0:T(8,128)(2,1)S(1)}, bf16[512,256]{1,0:T(8,128)(2,1)}, u32[]{:S(2)}) copy-start(bf16[512,256]{1,0:T(8,128)(2,1)} %constant.97.clone.zh_ref) | copy-start | bytes 786436
  308.6 99.2 %copy-start.3 = (bf16[512,256]{1,0:T(8,128)(2,1)S(1)}, bf16[512,256]{1,0:T(8,128)(2,1)}, u32[]{:S(2)}) copy-start(bf16[512,256]{1,0:T(8,128)(2,1)} %constant.98.clone.zl_ref) | copy-start | bytes 786436
  308.6 99.2 %copy-start.4 = (bf16[256,256]{1,0:T(8,128)(2,1)S(1)}, bf16[256,256]{1,0:T(8,128)(2,1)}, u32[]{:S(2)}) copy-start(bf16[256,256]{1,0:T(8,128)(2,1)} %constant.96.clone.restore_ref) | copy-start | bytes 393220
  308.6 99.2 %all-to-all-start.2 = ((bf16[8,32,64,256]{3,2,1,0:T(8,128)(2,1)}), bf16[8,32,64,256]{3,2,1,0:T(8,128)(2,1)}, u32[]{:S(2)}, u32[]{:S(2)}) async-start(bf16[8,32,64,256]{3,2,1,0:T(8,128)(2,1)} %planes.1), calls=%async_computation.2 | async-start | bytes 16777216 | tf_op jit(solution)/shard_map/all_to_all | solution.py:449
